TPU v7x, 32 devices: a whole 2x2x4 slice. The times are simulated.
32 devices in a mesh: groups: 2 (over y), rows: 8 (over z, x), layers: 2 (over core).
Axes of the slice: x: 2, y: 2, z: 4, core: 2. Of those that a mesh axis runs over, the one named last changes fastest.
Arguments:
- train_grads: bfloat16 [6144, 2, 4096], P(('groups', 'rows'), 'layers'), parts along dimension 0, may hold values from -6 to 6
- query_grads: bfloat16 [2, 2048, 4096], P('layers', ('groups', 'rows')), parts along dimension 1, may hold values from -0.09375 to 0.09375
Outputs:
- scores: float32 [1024, 6144], P('layers', ('groups', 'rows')), parts along dimension 1
There are 2 independent parts, one for each index of `groups`. A program takes and returns all parts, laid end to end along the dimension named above; each array names one. Nothing has to cross between parts.
All inputs are finite; a program needn't handle non-finite values.
Results may differ from a plain program's by a relative error of at most 0.0003.
Values may be sent and summed in bfloat16 or wider, within the bound.
A program may use at most 64 MiB of HBM per device.

v0:
```python
import jax
import jax.numpy as jnp
from jax import lax
from jax.sharding import PartitionSpec as P


def partial_scores(queries, train_grads):
    return jnp.einsum("lqk,nlk->qn", queries, train_grads, preferred_element_type=jnp.float32)


def shards(train_grads, query_grads):
    terms = partial_scores(lax.all_gather(query_grads, "rows", axis=1, tiled=True), train_grads)
    return lax.psum_scatter(terms, "layers", scatter_dimension=0, tiled=True)


def solution(mesh):
    in_specs = (P(("groups", "rows"), "layers", None), P("layers", ("groups", "rows"), None))
    out_specs = P("layers", ("groups", "rows"))
    return jax.shard_map(shards, mesh=mesh, in_specs=in_specs, out_specs=out_specs, check_vma=False)
```

profile of v0, /device:TPU:1, one launch (start us, length us, event | category | flops | bytes accessed | tf_op | source)
XLA Modules:
  0.0 159.3 jit_solution(11661200120718518420)
XLA Ops:
  6.5 0.0 copy-start
  6.5 0.0 all-gather.2.cloned.1.call-start
  6.5 0.7 all-gather.2.cloned.1.call-update
  7.3 0.0 reduce-scatter.2.cloned.1.call-start
  7.3 128.8 %all-gather.2.cloned.1.call-done = bf16[1,1024,4096]{2,1,0:T(8,128)(2,1)} async-done(((bf16[1,128,4096]{2,1,0:T(8,128)(2,1)}), bf16[1,1024,4096]{2,1,0:T(8,128)(2,1)}) %all-gather.2.cloned.1.call-update) | async-done | bytes 8388624 | tf_op jit(solution)/shard_map/all_gather | solution.py:12
  136.1 0.0 copy-done
  136.1 8.1 %fusion = f32[1024,384]{1,0:T(8,128)} fusion(bf16[1,1024,4096]{2,1,0:T(8,128)(2,1)} %all-gather.2.cloned.1.call-done, bf16[384,1,4096]{2,0,1:T(8,128)(2,1)S(1)} %copy-done), kind=kOutput, calls=%fused_computation | convolution fusion | flops 3221225472 | bytes 13107200 | tf_op jit(solution)/shard_map/lqk,nlk->qn/dot_general | solution.py:8
  144.3 0.0 reduce-scatter.2.cloned.1.call-update
  144.3 8.2 %reduce-scatter.2.cloned.1.call-done = f32[512,384]{1,0:T(8,128)} async-done(((f32[1024,384]{1,0:T(8,128)}), f32[512,384]{1,0:T(8,128)}) %reduce-scatter.2.cloned.1.call-update) | async-done | bytes 786448 | tf_op jit(solution)/shard_map/reduce_scatter | solution.py:13
Async XLA Ops:
  6.5 129.6 %copy-start = (bf16[384,1,4096]{2,0,1:T(8,128)(2,1)S(1)}, bf16[384,1,4096]{2,0,1:T(8,128)(2,1)}, u32[]{:S(2)}) copy-start(bf16[384,1,4096]{2,0,1:T(8,128)(2,1)} %param.2) | copy-start | bytes 9437188
  6.5 129.6 %all-gather.2.cloned.1.call-start = ((), (), s32[]{:S(2)}) async-start(), calls=%async_computation.1 | async-start | bytes 9437184 | tf_op jit(solution)/shard_map/all_gather | solution.py:12
  7.3 145.2 %reduce-scatter.2.cloned.1.call-start = ((), (), s32[]{:S(2)}) async-start(), calls=%async_computation.2 | async-start | bytes 2359296 | tf_op jit(solution)/shard_map/reduce_scatter | solution.py:13
Sparse Core Ops, SparseCore 0:
  9.5 126.5 all-gather.1
  144.4 8.0 reduce-scatter.1
where the time goes:
time: 160 us; the launch traced here: 159 us
  waiting for transfers between devices  138 us (86%)
  between operations  13.4 us (8%)
  matrix products  8.13 us (5%)
    all_gather x1, waiting for transfers between devices, shards(): lax.all_gather(query_grads, 'rows', axis=1, tiled=True)  129 us
    reduce_scatter x1, waiting for transfers between devices, shards(): return lax.psum_scatter(terms, 'layers', scatter_dimension=0, tiled=True)  8.21 us
    dot_general x1, matrix products, partial_scores(): jnp.einsum('lqk,nlk->qn', queries, train_grads, preferred_element_type=jn...  8.13 us
  transfers between devices with their start and end apart: 2, of which 2 were waited for; matrix products, arithmetic and copies ran while one was open for 0% of the time, Pallas kernels for 0%

commit v1 on v0

v1 whole, which is shorter than its diff:
```python
import functools
import math

import jax
import jax.numpy as jnp
from jax import lax
from jax.experimental import pallas as pl
from jax.experimental.pallas import tpu as pltpu
from jax.sharding import PartitionSpec as P

PARTS = 2
PIECES = 4
MESH = pl.DeviceIdType.MESH


def schedule(step, place, side, line, parts):
    subs = 2 * parts
    near = jnp.minimum(place, line - 1 - place)
    far = jnp.where(place < line - 1 - place, 1, -1)
    past = step - subs
    paired = past < 2 * near * subs
    within = lax.rem(past, 2 * subs)
    rest = past - 2 * near * subs
    apart = jnp.where(paired, past // (2 * subs) + 1, near + 1 + rest // subs)
    way = jnp.where(paired & (lax.rem(within, 2) == 1), -far, far)
    own = step < subs
    position = jnp.where(own, place, place + way * apart)
    turn = jnp.where(own, step, jnp.where(paired, within // 2, lax.rem(rest, subs)))
    shard = jnp.where(turn < parts, side, 1 - side)
    return position, shard, lax.rem(turn, parts)


def kernel(line, layers, parts, train, queries, out, qbuf, tbuf, pbuf, lbuf, rbuf,
           q_recv, q_send, x_send, t_recv, t_send, l_recv, l_send, r_recv, r_send):
    chunks, height, half = qbuf.shape
    rows = tbuf.shape[1]
    owned = rbuf.shape[0]
    subs = 2 * parts
    me = lax.axis_index("rows")
    layer = lax.axis_index("layers")
    place, side = me // 2, lax.rem(me, 2)
    other = 1 - side
    twin = me + 1 - 2 * side
    has_left, has_right = place > 0, place < line - 1
    left = jnp.where(has_left, me - 2, me)
    right = jnp.where(has_right, me + 2, me)
    pieces = t_recv.shape[0] - 1
    tall = rows // pieces
    mine = pl.ds(pl.multiple_of(side * half, half), half)
    theirs = pl.ds(pl.multiple_of(other * half, half), half)

    def name(position, shard, part):
        return (position * 2 + shard) * parts + part

    def visit(step):
        position, shard, part = schedule(step, place, side, line, parts)
        return position, name(position, shard, part)

    def remote(src, dst, send, recv, axis, device):
        return pltpu.make_async_remote_copy(
            src_ref=src, dst_ref=dst, send_sem=send, recv_sem=recv,
            device_id={axis: device}, device_id_type=MESH)

    def local_query(part):
        chunk = name(place, side, part)
        return pltpu.make_async_copy(
            queries.at[pl.ds(part * height, height), mine], qbuf.at[chunk], q_recv.at[chunk])

    def twin_query(part):
        chunk = name(place, side, part)
        return remote(queries.at[pl.ds(part * height, height), theirs], qbuf.at[chunk],
                      x_send.at[part], q_recv.at[chunk], "rows", twin)

    def own_query(part, way, device):
        chunk = name(place, side, part)
        return remote(queries.at[pl.ds(part * height, height), mine], qbuf.at[chunk],
                      q_send.at[way, chunk], q_recv.at[chunk], "rows", device)

    def forward(chunk, way, device):
        return remote(qbuf.at[chunk], qbuf.at[chunk], q_send.at[way, chunk], q_recv.at[chunk],
                      "rows", device)

    def twin_train(piece):
        return remote(train.at[pl.ds(piece * tall, tall), theirs],
                      tbuf.at[side, pl.ds(piece * tall, tall), :],
                      t_send.at[piece], t_recv.at[piece], "rows", twin)

    def local_train():
        return pltpu.make_async_copy(train.at[:, mine], tbuf.at[side], t_recv.at[pieces])

    def split(chunk):
        owner = chunk // owned
        return owner, chunk - owner * owned

    def to_layer(chunk):
        owner, index = split(chunk)
        return remote(pbuf.at[chunk], lbuf.at[layer, index], l_send.at[chunk],
                      l_recv.at[layer, index], "layers", owner)

    def to_twin(chunk):
        _, index = split(chunk)
        return remote(pbuf.at[chunk, other], rbuf.at[index], r_send.at[index], r_recv.at[index],
                      "rows", twin)

    barrier = pltpu.get_barrier_semaphore()
    pl.semaphore_signal(barrier, inc=1, device_id={"rows": twin}, device_id_type=MESH)

    @pl.when(has_left)
    def _():
        pl.semaphore_signal(barrier, inc=1, device_id={"rows": left}, device_id_type=MESH)

    @pl.when(has_right)
    def _():
        pl.semaphore_signal(barrier, inc=1, device_id={"rows": right}, device_id_type=MESH)

    for hop in range(1, layers):
        pl.semaphore_signal(barrier, inc=1, device_id={"layers": lax.rem(layer + hop, layers)},
                            device_id_type=MESH)
    for part in range(parts):
        local_query(part).start()
    local_train().start()
    pl.semaphore_wait(
        barrier, layers + has_left.astype(jnp.int32) + has_right.astype(jnp.int32))

    for part in range(parts):
        twin_query(part).start()

        @pl.when(has_left)
        def _():
            own_query(part, 0, left).start()

        @pl.when(has_right)
        def _():
            own_query(part, 1, right).start()

    def arrive(step):
        position, chunk = visit(step)
        own = step < parts
        forward(chunk, 0, twin).wait_recv()

        @pl.when((position >= place) & has_left & jnp.logical_not(own))
        def _():
            forward(chunk, 0, left).start()

        @pl.when((position <= place) & has_right & jnp.logical_not(own))
        def _():
            forward(chunk, 1, right).start()

    def loop(low, high, body):
        lax.fori_loop(low, high, lambda step, carry: (body(step), carry)[1], 0)

    loop(0, subs, arrive)
    for piece in range(pieces):
        twin_train(piece).start()
    early = jnp.where(has_left & has_right, chunks, chunks - subs)
    loop(subs, early, arrive)
    local_train().wait()
    for piece in range(pieces):
        remote(tbuf.at[other, pl.ds(piece * tall, tall), :], tbuf.at[other, pl.ds(piece * tall, tall), :],
               t_send.at[piece], t_recv.at[piece], "rows", twin).wait_recv()

    def product(step):
        @pl.when(step >= early)
        def _():
            arrive(step)

        _, chunk = visit(step)
        owner, _ = split(chunk)
        block = qbuf[chunk]
        for shard in range(2):
            pbuf[chunk, shard] = lax.dot_general(
                block, tbuf[shard], (((1,), (1,)), ((), ())), preferred_element_type=jnp.float32)

        @pl.when(owner != layer)
        def _():
            to_layer(chunk).start()

    def sum_layers(step):
        _, chunk = visit(step)
        owner, index = split(chunk)

        @pl.when(owner == layer)
        def _():
            for hop in range(1, layers):
                source = lax.rem(layer + hop, layers)
                remote(pbuf.at[chunk], lbuf.at[source, index], l_send.at[chunk],
                       l_recv.at[source, index], "rows", twin).wait_recv()
                for shard in range(2):
                    pbuf[chunk, shard] = pbuf[chunk, shard] + lbuf[source, index, shard]
            to_twin(chunk).start()

    def both(step):
        product(step)

        @pl.when(step > 0)
        def _():
            sum_layers(step - 1)

    loop(0, chunks, both)
    sum_layers(chunks - 1)

    def finish(step):
        position, chunk = visit(step)
        owner, index = split(chunk)

        @pl.when(owner == layer)
        def _():
            to_twin(chunk).wait_send()
            remote(rbuf.at[index], rbuf.at[index], r_send.at[index], r_recv.at[index],
                   "rows", twin).wait_recv()
            out[pl.ds(pl.multiple_of(index * height, height), height), :] = pbuf[chunk, side] + rbuf[index]

        @pl.when(owner != layer)
        def _():
            to_layer(chunk).wait_send()

        @pl.when((position >= place) & has_left)
        def _():
            forward(chunk, 0, left).wait_send()

        @pl.when((position <= place) & has_right)
        def _():
            forward(chunk, 1, right).wait_send()

    loop(0, chunks, finish)
    for part in range(parts):
        twin_query(part).wait_send()
    for piece in range(pieces):
        twin_train(piece).wait_send()


def solution(mesh):
    line, layers = mesh.shape["rows"] // 2, mesh.shape["layers"]

    def shards(train_grads, query_grads):
        train = train_grads.reshape(train_grads.shape[0], -1)
        queries = jnp.moveaxis(query_grads, 0, 1).reshape(query_grads.shape[1], -1)
        rows, depth = train.shape
        mine = queries.shape[0]
        every = mine * 2 * line
        share = every // layers
        height = math.gcd(math.gcd(mine, share), max(mine // PARTS, 64))
        parts, chunks, owned, half = mine // height, every // height, share // height, depth // 2
        pieces = PIECES if rows % (16 * PIECES) == 0 else 1
        dma = pltpu.SemaphoreType.DMA
        return pl.pallas_call(
            functools.partial(kernel, line, layers, parts),
            out_shape=jax.ShapeDtypeStruct((share, rows), jnp.float32),
            in_specs=[pl.BlockSpec(memory_space=pl.ANY)] * 2,
            out_specs=pl.BlockSpec(memory_space=pltpu.VMEM),
            scratch_shapes=[
                pltpu.VMEM((chunks, height, half), train.dtype),
                pltpu.VMEM((2, rows, half), train.dtype),
                pltpu.VMEM((chunks, 2, height, rows), jnp.float32),
                pltpu.VMEM((layers, owned, 2, height, rows), jnp.float32),
                pltpu.VMEM((owned, height, rows), jnp.float32),
                dma((chunks,)),
                dma((2, chunks)),
                dma((parts,)),
                dma((pieces + 1,)),
                dma((pieces,)),
                dma((layers, owned)),
                dma((chunks,)),
                dma((owned,)),
                dma((owned,)),
            ],
            compiler_params=pltpu.CompilerParams(
                collective_id=0, has_side_effects=True, vmem_limit_bytes=48 << 20),
            cost_estimate=pl.CostEstimate(
                flops=2 * every * rows * depth, transcendentals=0,
                bytes_accessed=2 * (rows + mine) * depth + 4 * share * rows),
        )(train, queries)

    in_specs = (P(("groups", "rows"), "layers", None), P("layers", ("groups", "rows"), None))
    out_specs = P("layers", ("groups", "rows"))
    return jax.shard_map(shards, mesh=mesh, in_specs=in_specs, out_specs=out_specs, check_vma=False)
```

time: 160 us -> 83 us (0.52)
  waiting for transfers between devices: 138 us -> 0 us
  Pallas kernels: 0 us -> 78.8 us
  between operations: 13.4 us -> 0.01 us
  matrix products: 8.13 us -> 0 us
  local copies, waits for them, and re-layouts: 0.01 us -> 4 us
    all_gather x1 -> x0, waiting for transfers between devices: 129 us -> none  [shards(): lax.all_gather(query_grads, 'rows', axis=1, tiled=True)]
    pallas_call x0 -> x1, Pallas kernels: none -> 78.8 us  [shards(): pl.pallas_call(functools.partial(kernel, line, layers, parts), out_shape=...]
    reduce_scatter x1 -> x0, waiting for transfers between devices: 8.21 us -> none  [shards(): return lax.psum_scatter(terms, 'layers', scatter_dimension=0, tiled=True)]
    dot_general x1 -> x0, matrix products: 8.13 us -> none  [partial_scores(): jnp.einsum('lqk,nlk->qn', queries, train_grads, preferred_element_type=jn...]
    unnamed x2 -> x5, local copies, waits for them, and re-layouts: 0.01 us -> 4 us
  transfers between devices with their start and end apart: 2 -> 0, of which waited for: 2 -> 0; matrix products, arithmetic and copies ran while one was open for 0% -> 0% of each run, Pallas kernels for 0% -> 0%
where the time goes in v1:
time: 83 us; the launch traced here: 82.8 us
  Pallas kernels  78.8 us (95%)
  local copies, waits for them, and re-layouts  4 us (5%)
    pallas_call x1, Pallas kernels, shards(): pl.pallas_call(functools.partial(kernel, line, layers, parts), out_shape=...  78.8 us
    unnamed x5, local copies, waits for them, and re-layouts  4 us

profile of v1, /device:TPU:1, one launch (start us, length us, event | category | flops | bytes accessed | tf_op | source)
XLA Modules:
  0.0 82.8 jit_solution(16989852101231955485)
XLA Ops:
  0.0 0.0 copy-start
  0.0 1.9 %copy-done = bf16[384,1,4096]{2,0,1:T(8,128)(2,1)S(1)} copy-done((bf16[384,1,4096]{2,0,1:T(8,128)(2,1)S(1)}, bf16[384,1,4096]{2,0,1:T(8,128)(2,1)}, u32[]{:S(2)}) %copy-start) | copy-done | bytes 3145752
  1.9 0.0 copy-start.1
  1.9 1.2 %copy-done.1 = bf16[1,128,4096]{2,1,0:T(8,128)(2,1)S(1)} copy-done((bf16[1,128,4096]{2,1,0:T(8,128)(2,1)S(1)}, bf16[1,128,4096]{2,1,0:T(8,128)(2,1)}, u32[]{:S(2)}) %copy-start.1) | copy-done | bytes 1048600
  3.1 78.8 %shard_map.28 = f32[512,384]{1,0:T(8,128)S(1)} custom-call(bf16[384,4096]{1,0:T(8,128)(2,1)S(1)} %bitcast.2, bf16[128,4096]{1,0:T(8,128)(2,1)S(1)} %bitcast.3), custom_call_target="tpu_custom_call" | custom-call | flops 3221225472 | bytes 4980736 | tf_op jit(solution)/shard_map/pallas_call | solution.py:246
  81.9 0.9 %copy.4 = f32[512,384]{1,0:T(8,128)} copy(f32[512,384]{1,0:T(8,128)S(1)} %shard_map.28) | data formatting | bytes 1572864
Async XLA Ops:
  0.0 1.9 %copy-start = (bf16[384,1,4096]{2,0,1:T(8,128)(2,1)S(1)}, bf16[384,1,4096]{2,0,1:T(8,128)(2,1)}, u32[]{:S(2)}) copy-start(bf16[384,1,4096]{2,0,1:T(8,128)(2,1)} %param.2) | copy-start | bytes 9437188
  1.9 1.2 %copy-start.1 = (bf16[1,128,4096]{2,1,0:T(8,128)(2,1)S(1)}, bf16[1,128,4096]{2,1,0:T(8,128)(2,1)}, u32[]{:S(2)}) copy-start(bf16[1,128,4096]{2,1,0:T(8,128)(2,1)} %param.3) | copy-start | bytes 3145732

commit v2 on v1

--- a/solution.py
+++ b/solution.py
@@ -152,31 +152,21 @@
     loop(0, subs, arrive)
     for piece in range(pieces):
         twin_train(piece).start()
-    early = jnp.where(has_left & has_right, chunks, chunks - subs)
-    loop(subs, early, arrive)
+    inner = has_left & has_right
+    loop(subs, jnp.where(inner, chunks, subs), arrive)
     local_train().wait()
     for piece in range(pieces):
         remote(tbuf.at[other, pl.ds(piece * tall, tall), :], tbuf.at[other, pl.ds(piece * tall, tall), :],
                t_send.at[piece], t_recv.at[piece], "rows", twin).wait_recv()
 
-    def product(step):
-        @pl.when(step >= early)
-        def _():
-            arrive(step)
-
-        _, chunk = visit(step)
+    def to_owner(chunk):
         owner, _ = split(chunk)
-        block = qbuf[chunk]
-        for shard in range(2):
-            pbuf[chunk, shard] = lax.dot_general(
-                block, tbuf[shard], (((1,), (1,)), ((), ())), preferred_element_type=jnp.float32)
 
         @pl.when(owner != layer)
         def _():
             to_layer(chunk).start()
 
-    def sum_layers(step):
-        _, chunk = visit(step)
+    def sum_layers(chunk):
         owner, index = split(chunk)
 
         @pl.when(owner == layer)
@@ -189,15 +179,44 @@
                     pbuf[chunk, shard] = pbuf[chunk, shard] + lbuf[source, index, shard]
             to_twin(chunk).start()
 
-    def both(step):
-        product(step)
-
-        @pl.when(step > 0)
-        def _():
-            sum_layers(step - 1)
-
-    loop(0, chunks, both)
-    sum_layers(chunks - 1)
+    def product(first, count):
+        block = qbuf[pl.ds(first, count)].reshape(count * height, half)
+        for shard in range(2):
+            terms = lax.dot_general(
+                block, tbuf[shard], (((1,), (1,)), ((), ())), preferred_element_type=jnp.float32)
+            pbuf[pl.ds(first, count), shard] = terms.reshape(count, height, rows)
+
+    def first_of(turn):
+        return subs * jnp.where(inner, turn, jnp.where(has_right, turn, line - 1 - turn))
+
+    def position(turn):
+        @pl.when(jnp.logical_not(inner) & (turn > 0))
+        def _():
+            loop(turn * subs, turn * subs + subs, arrive)
+
+        product(first_of(turn), subs)
+        for sub in range(subs):
+            to_owner(first_of(turn) + sub)
+
+        @pl.when(turn > 0)
+        def _():
+            for sub in range(subs):
+                sum_layers(first_of(turn - 1) + sub)
+
+    whole = jnp.where(inner, line, line - 1)
+    loop(0, whole, position)
+    for sub in range(subs):
+        sum_layers(first_of(whole - 1) + sub)
+
+    def last(step):
+        arrive(step)
+        _, chunk = visit(step)
+        product(chunk, 1)
+        to_owner(chunk)
+
+        @pl.when(step > chunks - subs)
+        def _():
+            sum_layers(visit(step - 1)[1])
 
     def finish(step):
         position, chunk = visit(step)
@@ -222,7 +241,14 @@
         def _():
             forward(chunk, 1, right).wait_send()
 
-    loop(0, chunks, finish)
+    @pl.when(jnp.logical_not(inner))
+    def _():
+        loop(chunks - subs, chunks - parts, last)
+        loop(0, chunks - subs, finish)
+        loop(chunks - parts, chunks, last)
+        sum_layers(visit(chunks - 1)[1])
+
+    loop(jnp.where(inner, 0, chunks - subs), chunks, finish)
     for part in range(parts):
         twin_query(part).wait_send()
     for piece in range(pieces):
@@ -265,7 +291,7 @@
                 dma((owned,)),
             ],
             compiler_params=pltpu.CompilerParams(
-                collective_id=0, has_side_effects=True, vmem_limit_bytes=48 << 20),
+                collective_id=0, has_side_effects=True, vmem_limit_bytes=55000000),
             cost_estimate=pl.CostEstimate(
                 flops=2 * every * rows * depth, transcendentals=0,
                 bytes_accessed=2 * (rows + mine) * depth + 4 * share * rows),

time: 83 us -> 80.1 us (0.965)
  local copies, waits for them, and re-layouts: 4 us -> 0.88 us
    unnamed x5 -> x1, local copies, waits for them, and re-layouts: 4 us -> 0.88 us
where the time goes in v2:
time: 80.1 us; the launch traced here: 79.9 us
  Pallas kernels  79 us (99%)
  local copies, waits for them, and re-layouts  0.88 us (1%)
    pallas_call x1, Pallas kernels, shards(): pl.pallas_call(functools.partial(kernel, line, layers, parts), out_shape=...  79 us

profile of v2, /device:TPU:1, one launch (start us, length us, event | category | flops | bytes accessed | tf_op | source)
XLA Modules:
  0.0 79.9 jit_solution(11004881444042610778)
XLA Ops:
  0.0 79.0 %shard_map.28 = f32[512,384]{1,0:T(8,128)S(1)} custom-call(bf16[384,4096]{1,0:T(8,128)(2,1)} %bitcast.2, bf16[128,4096]{1,0:T(8,128)(2,1)} %bitcast.3), custom_call_target="tpu_custom_call" | custom-call | flops 3221225472 | bytes 4980736 | tf_op jit(solution)/shard_map/pallas_call | solution.py:272
  79.0 0.9 %copy.4 = f32[512,384]{1,0:T(8,128)} copy(f32[512,384]{1,0:T(8,128)S(1)} %shard_map.28) | data formatting | bytes 1572864

commit v3 on v2

--- a/solution.py
+++ b/solution.py
@@ -40,6 +40,7 @@
     layer = lax.axis_index("layers")
     place, side = me // 2, lax.rem(me, 2)
     other = 1 - side
+    turns = (other, side)
     twin = me + 1 - 2 * side
     has_left, has_right = place > 0, place < line - 1
     left = jnp.where(has_left, me - 2, me)
@@ -92,10 +93,11 @@
         owner = chunk // owned
         return owner, chunk - owner * owned
 
-    def to_layer(chunk):
+    def to_layer(chunk, turn):
         owner, index = split(chunk)
-        return remote(pbuf.at[chunk], lbuf.at[layer, index], l_send.at[chunk],
-                      l_recv.at[layer, index], "layers", owner)
+        shard = turns[turn]
+        return remote(pbuf.at[chunk, shard], lbuf.at[layer, index, shard], l_send.at[turn, chunk],
+                      l_recv.at[turn, layer, index], "layers", owner)
 
     def to_twin(chunk):
         _, index = split(chunk)
@@ -159,32 +161,32 @@
         remote(tbuf.at[other, pl.ds(piece * tall, tall), :], tbuf.at[other, pl.ds(piece * tall, tall), :],
                t_send.at[piece], t_recv.at[piece], "rows", twin).wait_recv()
 
-    def to_owner(chunk):
-        owner, _ = split(chunk)
-
-        @pl.when(owner != layer)
-        def _():
-            to_layer(chunk).start()
-
     def sum_layers(chunk):
         owner, index = split(chunk)
 
         @pl.when(owner == layer)
         def _():
-            for hop in range(1, layers):
-                source = lax.rem(layer + hop, layers)
-                remote(pbuf.at[chunk], lbuf.at[source, index], l_send.at[chunk],
-                       l_recv.at[source, index], "rows", twin).wait_recv()
-                for shard in range(2):
+            for turn, shard in enumerate(turns):
+                for hop in range(1, layers):
+                    source = lax.rem(layer + hop, layers)
+                    remote(pbuf.at[chunk, shard], lbuf.at[source, index, shard], l_send.at[turn, chunk],
+                           l_recv.at[turn, source, index], "rows", twin).wait_recv()
                     pbuf[chunk, shard] = pbuf[chunk, shard] + lbuf[source, index, shard]
-            to_twin(chunk).start()
+                if turn == 0:
+                    to_twin(chunk).start()
 
     def product(first, count):
         block = qbuf[pl.ds(first, count)].reshape(count * height, half)
-        for shard in range(2):
+        for turn, shard in enumerate(turns):
             terms = lax.dot_general(
                 block, tbuf[shard], (((1,), (1,)), ((), ())), preferred_element_type=jnp.float32)
             pbuf[pl.ds(first, count), shard] = terms.reshape(count, height, rows)
+            for sub in range(count):
+                owner, _ = split(first + sub)
+
+                @pl.when(owner != layer)
+                def _():
+                    to_layer(first + sub, turn).start()
 
     def first_of(turn):
         return subs * jnp.where(inner, turn, jnp.where(has_right, turn, line - 1 - turn))
@@ -195,8 +197,6 @@
             loop(turn * subs, turn * subs + subs, arrive)
 
         product(first_of(turn), subs)
-        for sub in range(subs):
-            to_owner(first_of(turn) + sub)
 
         @pl.when(turn > 0)
         def _():
@@ -212,7 +212,6 @@
         arrive(step)
         _, chunk = visit(step)
         product(chunk, 1)
-        to_owner(chunk)
 
         @pl.when(step > chunks - subs)
         def _():
@@ -231,7 +230,8 @@
 
         @pl.when(owner != layer)
         def _():
-            to_layer(chunk).wait_send()
+            for turn in range(2):
+                to_layer(chunk, turn).wait_send()
 
         @pl.when((position >= place) & has_left)
         def _():
@@ -285,8 +285,8 @@
                 dma((parts,)),
                 dma((pieces + 1,)),
                 dma((pieces,)),
-                dma((layers, owned)),
-                dma((chunks,)),
+                dma((2, layers, owned)),
+                dma((2, chunks)),
                 dma((owned,)),
                 dma((owned,)),
             ],

time: 80.1 us -> 79.8 us (level)
  no operation moved by 1% of the time
where the time goes in v3:
time: 79.8 us; the launch traced here: 79.7 us
  Pallas kernels  78.8 us (99%)
  local copies, waits for them, and re-layouts  0.88 us (1%)
    pallas_call x1, Pallas kernels, shards(): pl.pallas_call(functools.partial(kernel, line, layers, parts), out_shape=...  78.8 us

profile of v3, /device:TPU:1, one launch (start us, length us, event | category | flops | bytes accessed | tf_op | source)
XLA Modules:
  0.0 79.7 jit_solution(10019955322300175066)
XLA Ops:
  0.0 78.8 %shard_map.28 = f32[512,384]{1,0:T(8,128)S(1)} custom-call(bf16[384,4096]{1,0:T(8,128)(2,1)} %bitcast.2, bf16[128,4096]{1,0:T(8,128)(2,1)} %bitcast.3), custom_call_target="tpu_custom_call" | custom-call | flops 3221225472 | bytes 4980736 | tf_op jit(solution)/shard_map/pallas_call | solution.py:272
  78.8 0.9 %copy.4 = f32[512,384]{1,0:T(8,128)} copy(f32[512,384]{1,0:T(8,128)S(1)} %shard_map.28) | data formatting | bytes 1572864

commit v4 on v3

--- a/solution.py
+++ b/solution.py
@@ -9,7 +9,7 @@
 from jax.sharding import PartitionSpec as P
 
 PARTS = 2
-PIECES = 4
+PIECES = 1
 MESH = pl.DeviceIdType.MESH
 
 
@@ -125,15 +125,15 @@
         barrier, layers + has_left.astype(jnp.int32) + has_right.astype(jnp.int32))
 
     for part in range(parts):
+        @pl.when(has_left)
+        def _():
+            own_query(part, 0, left).start()
+
+        @pl.when(has_right)
+        def _():
+            own_query(part, 1, right).start()
+
         twin_query(part).start()
-
-        @pl.when(has_left)
-        def _():
-            own_query(part, 0, left).start()
-
-        @pl.when(has_right)
-        def _():
-            own_query(part, 1, right).start()
 
     def arrive(step):
         position, chunk = visit(step)

time: 79.8 us -> 79.8 us (level)
  no operation moved by 1% of the time
where the time goes in v4:
time: 79.8 us; the launch traced here: 79.6 us
  Pallas kernels  78.8 us (99%)
  local copies, waits for them, and re-layouts  0.88 us (1%)
    pallas_call x1, Pallas kernels, shards(): pl.pallas_call(functools.partial(kernel, line, layers, parts), out_shape=...  78.8 us

profile of v4, /device:TPU:1, one launch (start us, length us, event | category | flops | bytes accessed | tf_op | source)
XLA Modules:
  0.0 79.6 jit_solution(7595995200728427756)
XLA Ops:
  0.0 78.8 %shard_map.28 = f32[512,384]{1,0:T(8,128)S(1)} custom-call(bf16[384,4096]{1,0:T(8,128)(2,1)} %bitcast.2, bf16[128,4096]{1,0:T(8,128)(2,1)} %bitcast.3), custom_call_target="tpu_custom_call" | custom-call | flops 3221225472 | bytes 4980736 | tf_op jit(solution)/shard_map/pallas_call | solution.py:272
  78.8 0.9 %copy.4 = f32[512,384]{1,0:T(8,128)} copy(f32[512,384]{1,0:T(8,128)S(1)} %shard_map.28) | data formatting | bytes 1572864
